TPU v7x, 512 devices: a whole 4x8x8 slice. The times are simulated.
512 devices in a mesh: seq: 32 (over y, x), head: 16 (over z, core).
Axes of the slice: x: 4, y: 8, z: 8, core: 2. Of those that a mesh axis runs over, the one named last changes fastest.
Arguments:
- queries: bfloat16 [2048, 8192], P('seq', 'head'), may hold values from -6 to 6
- keys: bfloat16 [2048, 1024], P('seq'), may hold values from -6 to 6
- values: bfloat16 [2048, 1024], P('seq'), may hold values from -6 to 6
- vertical: int32 [64, 8], replicated, may hold values from -1 to 31, as said below
- slash: int32 [64, 8], replicated, may hold values from -1 to 31, as said below
- plan: int32 [64], replicated, may hold values from 0 to 63, each once
Outputs:
- attended: bfloat16 [2048, 8192], P('seq', 'head')
Inputs may be any that keep to these rules, and one draw needn't show every extreme that they name: `vertical`: entries of 0 or more name key blocks of 64 positions; -1 marks an unused entry, and every row has at least one used entry. `slash`: entries of 0 or more are offsets back from a query's own block; -1 marks an unused entry; the first entry of every row is 0. `plan`: A permutation of the query heads.
All inputs are finite; a program needn't handle non-finite values.
Results may differ from a plain program's by a relative error of at most 0.0044.
Values may be sent and summed in bfloat16 or wider, within the bound.
A program may use at most 64 MiB of HBM per device.

v0:
```python
import jax
import jax.numpy as jnp
from jax import lax
from jax.sharding import PartitionSpec as P

HD = 128
QH = 64
KVH = 8
BLK = 64
floor_value = -1e30


def block_mask(query_blocks, key_blocks, vertical_rows, slash_rows, query_pos, key_pos):
    vertical_hit = jnp.any(vertical_rows[:, :, None] == key_blocks[None, None, :], axis=1)
    distance = query_blocks[:, None] - key_blocks[None, :]
    slash_hit = jnp.zeros((slash_rows.shape[0],) + distance.shape, jnp.bool_)
    for column in range(slash_rows.shape[1]):
        slash_hit = slash_hit | (slash_rows[:, column][:, None, None] == distance[None])
    causal = key_pos[None, :] <= query_pos[:, None]
    return causal[None] & (vertical_hit[:, None, :] | slash_hit)


def attend(carried, query_group, key_group, value_group, allowed, score_scale):
    max_old, totals_old, sums_old = carried
    scores = (
        jnp.einsum("qgh,kgh->gqk", query_group, key_group, preferred_element_type=jnp.float32)
        * score_scale
    )
    masked = jnp.where(allowed, scores, floor_value)
    max_new = jnp.maximum(max_old, jnp.max(masked, axis=2))
    weights = jnp.exp(masked - max_new[:, :, None])
    totals_new = jnp.sum(weights, axis=2)
    mixture = jnp.einsum(
        "gqk,kgh->qgh",
        weights.astype(jnp.bfloat16),
        value_group,
        preferred_element_type=jnp.float32,
    )
    return (max_new, totals_new, mixture)


def per_device(queries, keys, values, vertical, slash, plan):
    slot_count = plan.shape[0] // lax.axis_size("head")
    query_len = queries.shape[0]
    key_len = keys.shape[0]
    group_size = QH // KVH
    my_heads = lax.dynamic_slice_in_dim(plan, lax.axis_index("head") * slot_count, slot_count)
    kv_index = my_heads // group_size
    slot_column = jnp.arange(slot_count, dtype=jnp.int32)
    key_pick = jnp.take(keys.reshape(key_len, KVH, HD), kv_index, axis=1).reshape(
        key_len, slot_count * HD
    )
    value_pick = jnp.take(values.reshape(key_len, KVH, HD), kv_index, axis=1).reshape(
        key_len, slot_count * HD
    )
    gathered = lax.all_gather(queries, "head", axis=1, tiled=True)
    query_sel = jnp.take(gathered.reshape(query_len, QH, HD), my_heads, axis=1)
    vertical_sel = jnp.take(vertical, my_heads, axis=0)
    slash_sel = jnp.take(slash, my_heads, axis=0)
    query_pos = lax.axis_index("seq") * query_len + jnp.arange(query_len, dtype=jnp.int32)
    query_blocks = query_pos // BLK
    score_scale = HD ** (-0.5)

    def select_rows(rows):
        return jnp.take(rows.reshape(rows.shape[0], slot_count, HD), slot_column, axis=1)

    initial = (
        jnp.full((slot_count, query_len), floor_value, jnp.float32),
        jnp.zeros((slot_count, query_len), jnp.float32),
        jnp.zeros((query_len, slot_count, HD), jnp.float32),
    )
    key_piece = select_rows(lax.all_gather(key_pick, "seq", axis=0, tiled=True))
    value_piece = select_rows(lax.all_gather(value_pick, "seq", axis=0, tiled=True))
    piece_len = key_piece.shape[0]
    key_pos = jnp.arange(piece_len, dtype=jnp.int32)
    allowed = block_mask(query_blocks, key_pos // BLK, vertical_sel, slash_sel, query_pos, key_pos)
    max_parts = []
    total_parts = []
    sum_parts = []
    for lead in range(0, slot_count, 2):
        previous = (
            initial[0][lead : lead + 2],
            initial[1][lead : lead + 2],
            initial[2][:, lead : lead + 2],
        )
        updated = attend(
            previous,
            query_sel[:, lead : lead + 2],
            key_piece[:, lead : lead + 2],
            value_piece[:, lead : lead + 2],
            allowed[lead : lead + 2],
            score_scale,
        )
        max_parts.append(updated[0])
        total_parts.append(updated[1])
        sum_parts.append(updated[2])
    output = (
        jnp.concatenate(sum_parts, axis=1)
        / jnp.transpose(jnp.concatenate(total_parts, axis=0))[:, :, None]
    )
    return output.reshape(query_len, slot_count * HD).astype(jnp.bfloat16)


def solution(mesh):
    in_specs = (P("seq", "head"), P("seq", None), P("seq", None), P(), P(), P())
    out_specs = P("seq", "head")
    return jax.shard_map(
        per_device, mesh=mesh, in_specs=in_specs, out_specs=out_specs, check_vma=False
    )
```

profile of v0, /device:TPU:16, one launch (start us, length us, event | category | flops | bytes accessed | tf_op | source)
XLA Modules:
  0.0 250.0 jit_solution(17985091205724103392)
XLA Ops:
  6.5 0.7 all-gather.6.cloned.1.call-update
  7.3 0.7 compare_and_fusion
  8.1 0.6 gather_fusion.5
  8.7 0.9 copy_bitcast_fusion.1
  9.6 0.6 gather_fusion.1
  10.3 0.6 copy.48
  11.0 0.6 copy.49
  11.7 0.8 copy.28
  12.4 0.8 copy.29
  13.2 0.6 gather_fusion.3
  13.8 0.6 gather_fusion.4
  14.5 0.3 slice_reduce_fusion.7
  15.2 2.2 or_and_fusion
  17.4 38.6 %all-gather.6.cloned.1.call-done = bf16[64,8192]{1,0:T(8,128)(2,1)} async-done(((bf16[64,512]{1,0:T(8,128)(2,1)}), bf16[64,8192]{1,0:T(8,128)(2,1)}) %all-gather.6.cloned.1.call-update) | async-done | bytes 1048592 | tf_op jit(solution)/shard_map/all_gather | solution.py:56
  56.0 1.5 copy_bitcast_fusion
  57.5 0.6 gather_fusion
  58.1 82.0 %all-gather.4.cloned.1.call-done = bf16[2048,512]{1,0:T(8,128)(2,1)} async-done(((bf16[64,512]{1,0:T(8,128)(2,1)}), bf16[2048,512]{1,0:T(8,128)(2,1)}) %all-gather.4.cloned.1.call-update) | async-done | bytes 2097168 | tf_op jit(solution)/shard_map/all_gather | solution.py:73
  140.1 3.9 %copy.26 = bf16[2048,512]{0,1:T(8,128)(2,1)} copy(bf16[2048,512]{1,0:T(8,128)(2,1)} %all-gather.4.cloned.1.call-done) | data formatting | bytes 4194304 | tf_op jit(solution)/shard_map/all_gather | solution.py:73
  144.1 3.0 %copy.27 = bf16[2048,4,128]{2,0,1:T(8,128)(2,1)S(1)} copy(bf16[2048,4,128]{0,2,1:T(8,128)(2,1)} %bitcast.53) | data formatting | bytes 4194304 | tf_op jit(solution)/shard_map/reshape | solution.py:65
  147.1 76.9 %all-gather.8.cloned.1.call-done = bf16[2048,512]{1,0:T(8,128)(2,1)} async-done(((bf16[64,512]{1,0:T(8,128)(2,1)}), bf16[2048,512]{1,0:T(8,128)(2,1)}) %all-gather.8.cloned.1.call-update) | async-done | bytes 2097168 | tf_op jit(solution)/shard_map/all_gather | solution.py:72
  224.1 4.0 %copy.33 = bf16[2048,512]{0,1:T(8,128)(2,1)} copy(bf16[2048,512]{1,0:T(8,128)(2,1)} %all-gather.8.cloned.1.call-done) | data formatting | bytes 4194304 | tf_op jit(solution)/shard_map/all_gather | solution.py:72
  228.0 4.0 %copy.34 = bf16[2048,4,128]{2,0,1:T(8,128)(2,1)} copy(bf16[2048,4,128]{0,2,1:T(8,128)(2,1)} %bitcast.54) | data formatting | bytes 4194304 | tf_op jit(solution)/shard_map/reshape | solution.py:65
  232.0 2.1 gather_fusion.2
  234.1 3.9 %gather_fusion.6 = bf16[4,2048,128]{2,1,0:T(8,128)(2,1)} fusion(bf16[2048,4,128]{2,0,1:T(8,128)(2,1)} %copy.34, s32[1024]{0:T(1024)S(1)} %pad_clamp_fusion), kind=kCustom, calls=%fused_computation.4.clone | custom fusion | bytes 4194320 | tf_op jit(solution)/shard_map/jit(_take)/gather | solution.py:65
  238.0 2.0 select_bitcast_fusion.1
  240.0 0.6 fusion.23
  240.7 0.7 fusion.24
  241.3 0.3 fusion.8
  241.6 0.4 convolution_bitcast_fusion
  242.0 0.4 convolution_bitcast_fusion.1
  242.4 0.3 fusion.6
  242.8 0.7 copy_bitcast_fusion.3
  (25 shorter events, 0.8 us)
Async XLA Ops:
  6.5 1.5 copy-start
  6.5 49.5 %all-gather.6.cloned.1.call-start = ((), (), s32[]{:S(2)}) async-start(), calls=%async_computation.1 | async-start | bytes 1114112 | tf_op jit(solution)/shard_map/all_gather | solution.py:56
  7.3 132.9 %all-gather.4.cloned.1.call-start = ((), (), s32[]{:S(2)}) async-start(), calls=%async_computation | async-start | bytes 2162688 | tf_op jit(solution)/shard_map/all_gather | solution.py:73
  10.9 213.1 %all-gather.8.cloned.1.call-start = ((), (), s32[]{:S(2)}) async-start(), calls=%async_computation.2 | async-start | bytes 2162688 | tf_op jit(solution)/shard_map/all_gather | solution.py:72
  234.1 3.9 %copy-start.1 = (bf16[4,2048,128]{2,1,0:T(8,128)(2,1)S(1)}, bf16[4,2048,128]{2,1,0:T(8,128)(2,1)}, u32[]{:S(2)}) copy-start(bf16[4,2048,128]{2,1,0:T(8,128)(2,1)} %gather_fusion.2) | copy-start | bytes 6291460
Sparse Core Ops, SparseCore 0:
  9.5 46.4 all-gather.5
  59.2 80.8 all-gather.3
  143.3 80.7 all-gather.7
where the time goes:
time: 251 us; the launch traced here: 250 us
  waiting for transfers between devices  198 us (79%)
  local copies, waits for them, and re-layouts  29.3 us (12%)
  between operations  13.3 us (5%)
  other arithmetic  6.95 us (3%)
    all_gather x1, waiting for transfers between devices, per_device(): lax.all_gather(value_pick, 'seq', axis=0, tiled=True)  82 us
    all_gather x1, waiting for transfers between devices, per_device(): key_piece = select_rows(lax.all_gather(key_pick, 'seq', axis=0, tiled=True))  76.9 us
    all_gather x1, waiting for transfers between devices, per_device(): gathered = lax.all_gather(queries, 'head', axis=1, tiled=True)  38.6 us
    reshape x2, local copies, waits for them, and re-layouts, select_rows(): rows.reshape(rows.shape[0], slot_count, HD)  6.99 us
    gather x2, local copies, waits for them, and re-layouts, select_rows(): jnp.take(rows.reshape(rows.shape[0], slot_count, HD), slot_column, axis=1)  5.99 us
  transfers between devices with their start and end apart: 3, of which 3 were waited for; matrix products, arithmetic and copies ran while one was open for 8% of the time, Pallas kernels for 0%

commit v1 on v0

--- a/solution.py
+++ b/solution.py
@@ -8,6 +8,27 @@
 KVH = 8
 BLK = 64
 floor_value = -1e30
+
+
+def in_order(pieces, dim):
+    shape = list(pieces.shape[1:])
+    shape[dim] *= pieces.shape[0]
+    return jnp.moveaxis(pieces, 0, dim).reshape(shape)
+
+
+def doubled(x, axis):
+    devices, mine = (lax.axis_size(axis), lax.axis_index(axis))
+    parts, stride = (x[None], 1)
+    while stride < devices:
+        theirs = lax.ppermute(parts, axis, [(i, i ^ stride) for i in range(devices)])
+        low = mine & stride == 0
+        parts = jnp.concatenate([jnp.where(low, parts, theirs), jnp.where(low, theirs, parts)])
+        stride *= 2
+    return parts
+
+
+def doubled_up(x, axis, dim):
+    return in_order(doubled(x, axis), dim)
 
 
 def block_mask(query_blocks, key_blocks, vertical_rows, slash_rows, query_pos, key_pos):
@@ -69,7 +90,7 @@
         jnp.zeros((slot_count, query_len), jnp.float32),
         jnp.zeros((query_len, slot_count, HD), jnp.float32),
     )
-    key_piece = select_rows(lax.all_gather(key_pick, "seq", axis=0, tiled=True))
+    key_piece = select_rows(doubled_up(key_pick, "seq", 0))
     value_piece = select_rows(lax.all_gather(value_pick, "seq", axis=0, tiled=True))
     piece_len = key_piece.shape[0]
     key_pos = jnp.arange(piece_len, dtype=jnp.int32)

time: 251 us -> 181 us (0.72)
  waiting for transfers between devices: 198 us -> 106 us
  starting transfers between devices: 0.08 us -> 27.6 us
  local copies, waits for them, and re-layouts: 29.3 us -> 21.6 us
  other arithmetic: 6.95 us -> 9.83 us
    all_gather x1 -> x0, waiting for transfers between devices: 76.9 us -> none  [per_device(): key_piece = select_rows(lax.all_gather(key_pick, 'seq', axis=0, tiled=True))]
    ppermute x0 -> x5, waiting for transfers between devices: none -> 57.8 us  [doubled(): lax.ppermute(parts, axis, [(i, i ^ stride) for i in range(devices)])]
    all_gather x1, waiting for transfers between devices: 38.6 us -> 0.01 us  [per_device(): gathered = lax.all_gather(queries, 'head', axis=1, tiled=True)]
    all_gather x1, waiting for transfers between devices: 82 us -> 47.5 us  [per_device(): lax.all_gather(value_pick, 'seq', axis=0, tiled=True)]
    ppermute x0 -> x5, starting transfers between devices: none -> 27.6 us  [doubled(): lax.ppermute(parts, axis, [(i, i ^ stride) for i in range(devices)])]
    all_gather x1 -> x0, local copies, waits for them, and re-layouts: 3.97 us -> none  [per_device(): key_piece = select_rows(lax.all_gather(key_pick, 'seq', axis=0, tiled=True))]
    reshape x2 -> x1, local copies, waits for them, and re-layouts: 6.99 us -> 3.03 us  [select_rows(): rows.reshape(rows.shape[0], slot_count, HD)]
    another operation x0 -> x3, local copies, waits for them, and re-layouts: none -> 3.96 us  [the longest x2 3.93 us: select_rows(): rows.reshape(rows.shape[0], slot_count, HD)]
  transfers between devices with their start and end apart: 3 -> 7, of which waited for: 3 -> 6; matrix products, arithmetic and copies ran while one was open for 8% -> 10% of each run, Pallas kernels for 0% -> 0%
where the time goes in v1:
time: 181 us
  waiting for transfers between devices  106 us (59%)
  starting transfers between devices  27.6 us (15%)
  local copies, waits for them, and re-layouts  21.6 us (12%)
  between operations  13.7 us (8%)
  other arithmetic  9.83 us (5%)
  matrix products  2.08 us (1%)
    ppermute x5, waiting for transfers between devices, doubled(): lax.ppermute(parts, axis, [(i, i ^ stride) for i in range(devices)])  57.8 us
    all_gather x1, waiting for transfers between devices, per_device(): lax.all_gather(value_pick, 'seq', axis=0, tiled=True)  47.5 us
    ppermute x5, starting transfers between devices, doubled(): lax.ppermute(parts, axis, [(i, i ^ stride) for i in range(devices)])  27.6 us
    gather x2, local copies, waits for them, and re-layouts, select_rows(): jnp.take(rows.reshape(rows.shape[0], slot_count, HD), slot_column, axis=1)  4.28 us
    all_gather x1, local copies, waits for them, and re-layouts, per_device(): lax.all_gather(value_pick, 'seq', axis=0, tiled=True)  3.94 us
    another operation x2, local copies, waits for them, and re-layouts, select_rows(): rows.reshape(rows.shape[0], slot_count, HD)  3.93 us
  transfers between devices with their start and end apart: 7, of which 6 were waited for; matrix products, arithmetic and copies ran while one was open for 10% of the time, Pallas kernels for 0%

profile of v1, /device:TPU:16, one launch (start us, length us, event | category | flops | bytes accessed | tf_op | source)
XLA Modules:
  0.0 180.9 jit_solution(9348073325339976916)
XLA Ops:
  6.5 0.7 all-gather.5.cloned.1.call-update
  7.3 0.7 compare_and_fusion
  8.1 0.6 gather_fusion.1
  8.7 0.9 copy_bitcast_fusion.2
  9.6 0.6 gather_fusion.5
  10.4 3.4 %collective-permute-start = (bf16[1,64,512]{2,1,0:T(8,128)(2,1)S(1)}, bf16[1,64,512]{2,1,0:T(8,128)(2,1)S(1)}, u32[]{:S(2)}, u32[]{:S(2)}) collective-permute-start(bf16[1,64,512]{2,1,0:T(8,128)(2,1)S(1)} %broadcast_in_dim_reshape.3), channel_id=1, source_target_pairs={{0,16},{16,0},{32,48},{48,32},{64,80},{80,64},{96,112},{112,96},{1... | collective-permute-start | bytes 196616 | tf_op jit(solution)/shard_map/ppermute | solution.py:23
  13.8 0.6 copy.44
  14.5 2.1 %collective-permute-done = bf16[1,64,512]{2,1,0:T(8,128)(2,1)S(1)} collective-permute-done((bf16[1,64,512]{2,1,0:T(8,128)(2,1)S(1)}, bf16[1,64,512]{2,1,0:T(8,128)(2,1)S(1)}, u32[]{:S(2)}, u32[]{:S(2)}) %collective-permute-start) | collective-permute-done | bytes 65568 | tf_op jit(solution)/shard_map/ppermute | solution.py:23
  16.6 4.9 %collective-permute-start.1 = (bf16[2,64,512]{2,1,0:T(8,128)(2,1)S(1)}, bf16[2,64,512]{2,1,0:T(8,128)(2,1)S(1)}, u32[]{:S(2)}, u32[]{:S(2)}) collective-permute-start(bf16[2,64,512]{2,1,0:T(8,128)(2,1)S(1)} %pad_maximum_fusion.4), channel_id=1, source_target_pairs={{0,32},{16,48},{32,0},{48,16},{64,96},{80,112},{96,64},{112,80},{1... | collective-permute-start | bytes 393224 | tf_op jit(solution)/shard_map/ppermute | solution.py:23
  21.7 3.3 %collective-permute-done.1 = bf16[2,64,512]{2,1,0:T(8,128)(2,1)S(1)} collective-permute-done((bf16[2,64,512]{2,1,0:T(8,128)(2,1)S(1)}, bf16[2,64,512]{2,1,0:T(8,128)(2,1)S(1)}, u32[]{:S(2)}, u32[]{:S(2)}) %collective-permute-start.1) | collective-permute-done | bytes 131104 | tf_op jit(solution)/shard_map/ppermute | solution.py:23
  25.0 3.5 %collective-permute-start.2 = (bf16[4,64,512]{2,1,0:T(8,128)(2,1)S(1)}, bf16[4,64,512]{2,1,0:T(8,128)(2,1)S(1)}, u32[]{:S(2)}, u32[]{:S(2)}) collective-permute-start(bf16[4,64,512]{2,1,0:T(8,128)(2,1)S(1)} %pad_maximum_fusion.3), channel_id=1, source_target_pairs={{0,64},{16,80},{32,96},{48,112},{64,0},{80,16},{96,32},{112,48},{1... | collective-permute-start | bytes 786440 | tf_op jit(solution)/shard_map/ppermute | solution.py:23
  28.7 0.6 gather_fusion.3
  29.9 3.4 %collective-permute-done.2 = bf16[4,64,512]{2,1,0:T(8,128)(2,1)S(1)} collective-permute-done((bf16[4,64,512]{2,1,0:T(8,128)(2,1)S(1)}, bf16[4,64,512]{2,1,0:T(8,128)(2,1)S(1)}, u32[]{:S(2)}, u32[]{:S(2)}) %collective-permute-start.2) | collective-permute-done | bytes 262176 | tf_op jit(solution)/shard_map/ppermute | solution.py:23
  33.4 8.2 %collective-permute-start.3 = (bf16[8,64,512]{2,1,0:T(8,128)(2,1)S(1)}, bf16[8,64,512]{2,1,0:T(8,128)(2,1)S(1)}, u32[]{:S(2)}, u32[]{:S(2)}) collective-permute-start(bf16[8,64,512]{2,1,0:T(8,128)(2,1)S(1)} %pad_maximum_fusion.2), channel_id=1, source_target_pairs={{0,128},{16,144},{32,160},{48,176},{64,192},{80,208},{96,224},{112... | collective-permute-start | bytes 1572872 | tf_op jit(solution)/shard_map/ppermute | solution.py:23
  41.7 13.0 %collective-permute-done.3 = bf16[8,64,512]{2,1,0:T(8,128)(2,1)S(1)} collective-permute-done((bf16[8,64,512]{2,1,0:T(8,128)(2,1)S(1)}, bf16[8,64,512]{2,1,0:T(8,128)(2,1)S(1)}, u32[]{:S(2)}, u32[]{:S(2)}) %collective-permute-start.3) | collective-permute-done | bytes 524320 | tf_op jit(solution)/shard_map/ppermute | solution.py:23
  54.8 1.1 pad_maximum_fusion.1
  55.8 7.6 %collective-permute-start.4 = (bf16[16,64,512]{2,1,0:T(8,128)(2,1)}, bf16[16,64,512]{2,1,0:T(8,128)(2,1)S(1)}, u32[]{:S(2)}, u32[]{:S(2)}) collective-permute-start(bf16[16,64,512]{2,1,0:T(8,128)(2,1)} %pad_maximum_fusion.1), channel_id=1, source_target_pairs={{0,256},{16,272},{32,288},{48,304},{64,320},{80,336},{96,352},{112... | collective-permute-start | bytes 3145736 | tf_op jit(solution)/shard_map/ppermute | solution.py:23
  63.9 2.8 %or_and_fusion = pred[4,64,2048]{2,1,0:T(32,128)(4,1)} fusion(s32[64,2048]{1,0:T(8,128)S(1)} %broadcast_subtract_fusion, s32[4]{0:T(128)S(1)} %get-tuple-element.8, s32[4]{0:T(128)S(1)} %get-tuple-element.10, s32[4]{0:T(128)S(1)} %get-tuple-element.11, s32[4]{0:T(128)S(1)} %get-tuple-element.12, s32[4]{0:T(128)S(1)} %get-tuple-element.13, ...), kind=kLoop, calls=%fused_computation.14 | loop fusion | flops 8912896 | bytes 1187968 | tf_op jit(solution)/shard_map/and | solution.py:41
  66.7 1.5 copy_bitcast_fusion
  68.2 0.6 gather_fusion
  68.8 36.1 %collective-permute-done.4 = bf16[16,64,512]{2,1,0:T(8,128)(2,1)S(1)} collective-permute-done((bf16[16,64,512]{2,1,0:T(8,128)(2,1)}, bf16[16,64,512]{2,1,0:T(8,128)(2,1)S(1)}, u32[]{:S(2)}, u32[]{:S(2)}) %collective-permute-start.4) | collective-permute-done | bytes 1048608 | tf_op jit(solution)/shard_map/ppermute | solution.py:23
  105.2 2.1 %reshape_reshape.3 = bf16[2048,4,128]{2,1,0:T(4,128)(2,1)} reshape(bf16[32,64,512]{2,1,0:T(8,128)(2,1)S(1)} %pad_maximum_fusion) | data formatting | bytes 4194304 | tf_op jit(solution)/shard_map/reshape;reshape | solution.py:86
  107.3 1.9 %copy.32 = bf16[2048,4,128]{2,0,1:T(8,128)(2,1)S(1)} copy(bf16[2048,4,128]{2,1,0:T(4,128)(2,1)} %reshape_reshape.3) | data formatting | bytes 4194304 | tf_op jit(solution)/shard_map/reshape;reshape | solution.py:86
  109.1 2.1 %gather_fusion.6 = bf16[4,2048,128]{2,1,0:T(8,128)(2,1)} fusion(bf16[2048,4,128]{2,0,1:T(8,128)(2,1)S(1)} %copy.32, s32[1024]{0:T(1024)S(1)} %pad_clamp_fusion), kind=kCustom, calls=%fused_computation.4.clone | custom fusion | bytes 4194320 | tf_op jit(solution)/shard_map/jit(_take)/gather | solution.py:86
  111.2 47.5 %all-gather.3.cloned.1.call-done = bf16[2048,512]{1,0:T(8,128)(2,1)} async-done(((bf16[64,512]{1,0:T(8,128)(2,1)}), bf16[2048,512]{1,0:T(8,128)(2,1)}) %all-gather.3.cloned.1.call-update) | async-done | bytes 2097168 | tf_op jit(solution)/shard_map/all_gather | solution.py:94
  158.7 3.9 %copy.25 = bf16[2048,512]{0,1:T(8,128)(2,1)} copy(bf16[2048,512]{1,0:T(8,128)(2,1)} %all-gather.3.cloned.1.call-done) | data formatting | bytes 4194304 | tf_op jit(solution)/shard_map/all_gather | solution.py:94
  162.7 3.0 %copy.26 = bf16[2048,4,128]{2,0,1:T(8,128)(2,1)S(1)} copy(bf16[2048,4,128]{0,2,1:T(8,128)(2,1)} %bitcast.48) | data formatting | bytes 4194304 | tf_op jit(solution)/shard_map/reshape | solution.py:86
  165.7 2.2 %gather_fusion.2 = bf16[4,2048,128]{2,1,0:T(8,128)(2,1)} fusion(bf16[2048,4,128]{2,0,1:T(8,128)(2,1)S(1)} %copy.26, s32[1024]{0:T(1024)S(1)} %pad_clamp_fusion), kind=kCustom, calls=%fused_computation.1.clone | custom fusion | bytes 4194320 | tf_op jit(solution)/shard_map/jit(_take)/gather | solution.py:86
  167.9 2.7 %select_bitcast_fusion.1 = (bf16[2048,4,128]{2,0,1:T(8,128)(2,1)S(1)}, bf16[2048,4,128]{2,0,1:T(8,128)(2,1)S(1)}) fusion(bf16[4,2048,128]{2,1,0:T(8,128)(2,1)} %gather_fusion.2, pred[4]{0:T(512)(128)(4,1)S(1)} %iota_compare_fusion.1, bf16[4,2048,128]{2,1,0:T(8,128)(2,1)} %gather_fusion.6), kind=kLoop, calls=%fused_computation.13 | loop fusion | flops 2097152 | bytes 8388612 | tf_op jit(solution)/shard_map/jit(_take)/select_n | solution.py:86
  170.6 0.6 fusion.23
  171.3 0.7 fusion.24
  173.3 0.7 copy_bitcast_fusion.3
  (47 shorter events, 3.8 us)
Async XLA Ops:
  6.5 1.5 copy-start
  6.5 22.0 %copy-start.2 = (s32[64,8]{0,1:T(8,128)S(1)}, s32[64,8]{0,1:T(8,128)}, u32[]{:S(2)}) copy-start(s32[64,8]{0,1:T(8,128)} %param.15) | copy-start | bytes 6148
  6.5 22.1 %copy-start.3 = (s32[64,8]{0,1:T(8,128)S(1)}, s32[64,8]{0,1:T(8,128)}, u32[]{:S(2)}) copy-start(s32[64,8]{0,1:T(8,128)} %param.16) | copy-start | bytes 6148
  6.5 60.2 %all-gather.5.cloned.1.call-start = ((), (), s32[]{:S(2)}) async-start(), calls=%async_computation.1 | async-start | bytes 1114112 | tf_op jit(solution)/shard_map/all_gather | solution.py:77
  7.3 151.5 %all-gather.3.cloned.1.call-start = ((), (), s32[]{:S(2)}) async-start(), calls=%async_computation | async-start | bytes 2162688 | tf_op jit(solution)/shard_map/all_gather | solution.py:94
  10.4 6.2 %collective-permute-start = (bf16[1,64,512]{2,1,0:T(8,128)(2,1)S(1)}, bf16[1,64,512]{2,1,0:T(8,128)(2,1)S(1)}, u32[]{:S(2)}, u32[]{:S(2)}) collective-permute-start(bf16[1,64,512]{2,1,0:T(8,128)(2,1)S(1)} %broadcast_in_dim_reshape.3), channel_id=1, source_target_pairs={{0,16},{16,0},{32,48},{48,32},{64,80},{80,64},{96,112},{112,96},{1... | collective-permute-start | bytes 196616 | tf_op jit(solution)/shard_map/ppermute | solution.py:23
  16.6 8.4 %collective-permute-start.1 = (bf16[2,64,512]{2,1,0:T(8,128)(2,1)S(1)}, bf16[2,64,512]{2,1,0:T(8,128)(2,1)S(1)}, u32[]{:S(2)}, u32[]{:S(2)}) collective-permute-start(bf16[2,64,512]{2,1,0:T(8,128)(2,1)S(1)} %pad_maximum_fusion.4), channel_id=1, source_target_pairs={{0,32},{16,48},{32,0},{48,16},{64,96},{80,112},{96,64},{112,80},{1... | collective-permute-start | bytes 393224 | tf_op jit(solution)/shard_map/ppermute | solution.py:23
  25.0 8.3 %collective-permute-start.2 = (bf16[4,64,512]{2,1,0:T(8,128)(2,1)S(1)}, bf16[4,64,512]{2,1,0:T(8,128)(2,1)S(1)}, u32[]{:S(2)}, u32[]{:S(2)}) collective-permute-start(bf16[4,64,512]{2,1,0:T(8,128)(2,1)S(1)} %pad_maximum_fusion.3), channel_id=1, source_target_pairs={{0,64},{16,80},{32,96},{48,112},{64,0},{80,16},{96,32},{112,48},{1... | collective-permute-start | bytes 786440 | tf_op jit(solution)/shard_map/ppermute | solution.py:23
  33.4 21.3 %collective-permute-start.3 = (bf16[8,64,512]{2,1,0:T(8,128)(2,1)S(1)}, bf16[8,64,512]{2,1,0:T(8,128)(2,1)S(1)}, u32[]{:S(2)}, u32[]{:S(2)}) collective-permute-start(bf16[8,64,512]{2,1,0:T(8,128)(2,1)S(1)} %pad_maximum_fusion.2), channel_id=1, source_target_pairs={{0,128},{16,144},{32,160},{48,176},{64,192},{80,208},{96,224},{112... | collective-permute-start | bytes 1572872 | tf_op jit(solution)/shard_map/ppermute | solution.py:23
  55.8 49.0 %collective-permute-start.4 = (bf16[16,64,512]{2,1,0:T(8,128)(2,1)}, bf16[16,64,512]{2,1,0:T(8,128)(2,1)S(1)}, u32[]{:S(2)}, u32[]{:S(2)}) collective-permute-start(bf16[16,64,512]{2,1,0:T(8,128)(2,1)} %pad_maximum_fusion.1), channel_id=1, source_target_pairs={{0,256},{16,272},{32,288},{48,304},{64,320},{80,336},{96,352},{112... | collective-permute-start | bytes 3145736 | tf_op jit(solution)/shard_map/ppermute | solution.py:23
  167.9 2.7 %copy-start.1 = (pred[4,64,2048]{2,1,0:T(32,128)(4,1)S(1)}, pred[4,64,2048]{2,1,0:T(32,128)(4,1)}, u32[]{:S(2)}) copy-start(pred[4,64,2048]{2,1,0:T(32,128)(4,1)} %or_and_fusion) | copy-start | bytes 1572868
Sparse Core Ops, SparseCore 0:
  9.5 46.5 all-gather.4
  59.2 99.4 all-gather.2
